TPU v7x, 256 devices: a whole 4x4x8 slice. The times are simulated.
256 devices in a mesh: keys: 64 (over y, z, core), seq: 4 (over x).
Axes of the slice: x: 4, y: 4, z: 8, core: 2. Of those that a mesh axis runs over, the one named last changes fastest.
Arguments:
- span_queries: bfloat16 [1536, 768], P(('keys', 'seq')), may hold values from -6 to 6
- key_slab: bfloat16 [4096, 768], P('keys'), may hold values from -0.21875 to 0.21875
- neighbour_store: bfloat16 [4096, 64, 896], P('keys'), may hold values from -6 to 6
- neighbour_ids: int32 [1536, 2], P(('keys', 'seq')), may hold values from 0 to 4094, as said below
- attn_queries: bfloat16 [98304, 2048], P(('keys', 'seq')), may hold values from -200 to 200
- kv_weight: bfloat16 [2, 2048, 896], P(None, 'keys'), may hold values from -0.1875 to 0.1875
Outputs:
- best_scores: float32 [1536, 2], P(('keys', 'seq'))
- attended: bfloat16 [98304, 2048], P(('keys', 'seq'))
Inputs may be any that keep to these rules, and one draw needn't show every extreme that they name: `neighbour_ids`: each id c has c mod 64 at most 62, so c + 1 lies on the same shard c // 64. Among the 12 ids of one device's spans (aligned blocks of 6 rows), no shard holds more than 1, and some shard holds exactly 1.
All inputs are finite; a program needn't handle non-finite values.
Results may differ from a plain program's by a relative error of at most 0.012.
The roundings to bfloat16 on the way count: a program that leaves them out, or rounds other values in their place, can miss the bound.
Values may be sent and summed in bfloat16 or wider, within the bound.
A program may use at most 128 MiB of HBM per device.

v0:
```python
import jax
import jax.numpy as jnp
from jax import lax
from jax.sharding import PartitionSpec as P

HEADS = 16
HEAD_DIM = 128


def merged(part, axis, combine):
    gathered = jax.tree.map(lambda a: lax.all_gather(a, axis), part)

    def take(source):
        return jax.tree.map(lambda a: lax.dynamic_index_in_dim(a, source, 0, False), gathered)

    return lax.fori_loop(
        1, lax.axis_size(axis), lambda source, state: combine(state, take(source)), take(0)
    )


def keep_two(left, right):
    higher = jnp.maximum(left[0], right[0])
    runner = jnp.maximum(jnp.minimum(left[0], right[0]), jnp.maximum(left[1], right[1]))
    return (higher, runner)


def best_two(values):
    padding = jnp.full((values.shape[0], 2), -jnp.inf, values.dtype)
    return lax.top_k(jnp.concatenate([values, padding], axis=1), 2)[0]


def row_scores(left, right):
    return lax.dot_general(
        left, right, (((1,), (1,)), ((), ())), preferred_element_type=jnp.float32
    )


def body(span_queries, key_slab, neighbour_store, neighbour_ids, attn_queries, kv_weight):
    key_count = lax.axis_size("keys")
    position = lax.axis_index("keys")
    own_spans = neighbour_ids.shape[0]
    shard_spans = neighbour_store.shape[0]
    span_rows = neighbour_store.shape[1]
    enc_width = neighbour_store.shape[2]
    candidates = best_two(
        row_scores(lax.all_gather(span_queries, "keys", axis=0, tiled=True), key_slab)
    )
    higher_all, runner_all = merged((candidates[:, 0], candidates[:, 1]), "keys", keep_two)
    higher = lax.dynamic_slice_in_dim(higher_all, position * own_spans, own_spans)
    runner = lax.dynamic_slice_in_dim(runner_all, position * own_spans, own_spans)
    best_scores = jnp.stack([higher, runner], axis=1)
    flat_ids = neighbour_ids.reshape(-1)
    need_count = flat_ids.shape[0]
    per_shard = (need_count + key_count - 1) // key_count
    capacity = 2 * per_shard
    target = flat_ids // shard_spans
    offset = flat_ids % shard_spans
    order_index = jnp.arange(need_count, dtype=jnp.int32)
    same_shard = (target[:, None] == target[None, :]) & (
        order_index[:, None] < order_index[None, :]
    )
    slot_base = 2 * jnp.sum(same_shard.astype(jnp.int32), axis=0)
    slot_index = jnp.arange(capacity, dtype=jnp.int32)
    shard_onehot = (target[:, None] == jnp.arange(key_count, dtype=jnp.int32)[None, :]).astype(
        jnp.int32
    )
    first_slot = (slot_index == slot_base[..., None]).astype(jnp.int32) * offset[..., None]
    next_slot = (slot_index == slot_base[..., None] + 1).astype(jnp.int32) * (offset[..., None] + 1)
    table = jnp.einsum("nj,ns->js", shard_onehot, first_slot + next_slot)
    incoming = lax.all_to_all(table, "keys", split_axis=0, concat_axis=0, tiled=True)
    outgoing = neighbour_store[incoming]
    arrived = lax.all_to_all(outgoing, "keys", split_axis=0, concat_axis=0, tiled=True)
    arrived = arrived.reshape(key_count * capacity, span_rows, enc_width)
    first_row = target * capacity + slot_base
    picked = arrived[jnp.stack([first_row, first_row + 1], axis=1)]
    neighbours = picked.reshape(own_spans * 4 * span_rows, enc_width)
    keys_values = jnp.einsum(
        "re,tce->rtc",
        neighbours,
        lax.all_gather(kv_weight, "keys", axis=1, tiled=True),
        preferred_element_type=jnp.float32,
    ).astype(jnp.bfloat16)
    key_rows = keys_values[:, 0].reshape(own_spans, 4 * span_rows, HEADS, HEAD_DIM)
    value_rows = keys_values[:, 1].reshape(own_spans, 4 * span_rows, HEADS, HEAD_DIM)
    queries = attn_queries.reshape(own_spans, span_rows, HEADS, HEAD_DIM)
    logits = jnp.einsum(
        "cqhd,ckhd->chqk", queries, key_rows, preferred_element_type=jnp.float32
    ) * HEAD_DIM ** (-0.5)
    largest = jnp.max(logits, axis=-1, keepdims=True)
    expo_terms = jnp.exp(logits - largest)
    weights = (expo_terms / jnp.sum(expo_terms, axis=-1, keepdims=True)).astype(jnp.bfloat16)
    output = jnp.einsum("chqk,ckhd->cqhd", weights, value_rows, preferred_element_type=jnp.float32)
    attended = output.astype(jnp.bfloat16).reshape(own_spans * span_rows, HEADS * HEAD_DIM)
    return (best_scores, attended)


def solution(mesh):
    return jax.shard_map(
        body,
        mesh=mesh,
        in_specs=(
            P(("keys", "seq"), None),
            P("keys", None),
            P("keys", None, None),
            P(("keys", "seq"), None),
            P(("keys", "seq"), None),
            P(None, "keys", None),
        ),
        out_specs=(P(("keys", "seq"), None), P(("keys", "seq"), None)),
        check_vma=False,
    )
```

profile of v0, /device:TPU:1, one launch (start us, length us, event | category | flops | bytes accessed | tf_op | source)
XLA Modules:
  0.0 606.7 jit_solution(17030885371384447195)
XLA Ops:
  7.2 0.8 copy.33
  8.5 22.2 %all_to_all.17 = s32[64,1,2]{2,1,0:T(1,128)S(1)} all-to-all(s32[64,1,2]{2,1,0:T(1,128)S(1)} %bitcast.81), channel_id=1, replica_groups=mesh['keys'=64,'seq'=4] {'keys'}, dimensions={0} | all-to-all | bytes 1024 | tf_op jit(solution)/shard_map/all_to_all | solution.py:70
  31.1 11.9 %gather_fusion = bf16[128,64,896]{2,1,0:T(8,128)(2,1)} fusion(bf16[64,64,896]{2,1,0:T(8,128)(2,1)} %param.10, s32[1024]{0:T(1024)S(1)} %pad_clamp_fusion.1), kind=kCustom, calls=%fused_computation | custom fusion | bytes 29360640 | tf_op jit(solution)/shard_map/gather | solution.py:71
  43.0 6.2 %all-to-all-start.1 = ((bf16[64,2,64,896]{3,2,1,0:T(8,128)(2,1)}), bf16[64,2,64,896]{3,2,1,0:T(8,128)(2,1)}, u32[]{:S(2)}, u32[]{:S(2)}) async-start(bf16[64,2,64,896]{3,2,1,0:T(8,128)(2,1)} %bitcast.73), calls=%async_computation.1 | async-start | bytes 29360128 | tf_op jit(solution)/shard_map/all_to_all | solution.py:72
  49.3 0.7 all-gather.5.cloned.1.call-update
  50.3 1.6 copy.44
  51.8 380.2 %all-gather.2 = bf16[64,6,768]{2,1,0:T(8,128)(2,1)S(1)} all-gather(bf16[1,6,768]{2,1,0:T(8,128)(2,1)S(1)} %bitcast.82), channel_id=1, replica_groups=mesh['keys'=64,'seq'=4] {'keys'}, dimensions={0}, use_global_device_ids=true | all-gather | bytes 599040 | tf_op jit(solution)/shard_map/all_gather | solution.py:46
  432.5 5.0 top_k.8
  437.6 48.6 %all-gather = f32[24576,1]{0,1:T(1,128)S(1)} all-gather(f32[384,1]{0,1:T(1,128)S(1)} %get-tuple-element.161), channel_id=2, replica_groups=mesh['keys'=64,'seq'=4] {'keys'}, dimensions={0}, use_global_device_ids=true | all-gather | bytes 99840 | tf_op jit(solution)/shard_map/all_gather | solution.py:11
  486.7 0.9 reduce.14
  487.6 44.4 %all-gather.1 = f32[24576,1]{0,1:T(1,128)S(1)} all-gather(f32[384,1]{0,1:T(1,128)S(1)} %get-tuple-element.160), channel_id=3, replica_groups=mesh['keys'=64,'seq'=4] {'keys'}, dimensions={0}, use_global_device_ids=true | all-gather | bytes 99840 | tf_op jit(solution)/shard_map/all_gather | solution.py:11
  532.0 0.9 reduce.15
  533.0 4.3 while.17
  537.4 0.6 pad_maximum_fusion
  538.0 6.3 %gather_fusion.1 = bf16[24,64,896]{2,1,0:T(8,128)(2,1)S(1)} fusion(bf16[128,64,896]{2,1,0:T(8,128)(2,1)} %bitcast.6, s32[1024]{0:T(1024)S(1)} %pad_clamp_fusion), kind=kCustom, calls=%fused_computation.1 | custom fusion | bytes 5505120 | tf_op jit(solution)/shard_map/gather | solution.py:75
  544.3 18.7 %convolution_convert_fusion = bf16[1536,2,2048]{2,0,1:T(8,128)(2,1)} fusion(bf16[1536,896,1]{1,0,2:T(8,128)(2,1)S(1)} %bitcast.78, bf16[2,2048,896]{2,1,0:T(8,128)(2,1)} %all-gather.5.cloned.1.call-done), kind=kOutput, calls=%fused_computation.6 | convolution fusion | flops 11280580608 | bytes 22675456 | tf_op jit(solution)/shard_map/re,tce->rtc/dot_general | solution.py:77
  563.0 5.3 slice_bitcast_fusion.1
  568.3 2.3 copy.43
  570.7 3.7 fusion.5
  574.4 2.4 fusion.42
  576.8 5.0 copy.45
  581.8 15.5 %fusion.16 = bf16[6,64,16,128]{3,1,2,0:T(8,128)(2,1)S(1)} fusion(bf16[6,256,16,128]{3,2,1,0:T(8,128)(2,1)} %bitcast.75, f32[6,16,64]{2,1,0:T(8,128)S(1)} %fusion.42, f32[6,16,256,64]{2,3,1,0:T(8,128)} %copy-done.2), kind=kOutput, calls=%fused_computation.24 | convolution fusion | flops 411310336 | bytes 14180352 | tf_op jit(solution)/shard_map/chqk,ckhd->cqhd/dot_general | solution.py:92
  597.3 1.0 copy.42
  598.4 1.6 copy.58
  (166 shorter events, 4.9 us)
Async XLA Ops:
  7.2 425.0 %copy-start = (bf16[64,768]{1,0:T(8,128)(2,1)S(1)}, bf16[64,768]{1,0:T(8,128)(2,1)}, u32[]{:S(2)}) copy-start(bf16[64,768]{1,0:T(8,128)(2,1)} %param.9) | copy-start | bytes 294916
  43.0 7.3 %copy-start.3 = (bf16[384,2048]{1,0:T(8,128)(2,1)S(1)}, bf16[384,2048]{1,0:T(8,128)(2,1)}, u32[]{:S(2)}) copy-start(bf16[384,2048]{1,0:T(8,128)(2,1)} %param.12) | copy-start | bytes 4718596
  43.0 8.8 %copy-start.4 = (bf16[6,768]{1,0:T(8,128)(2,1)S(1)}, bf16[6,768]{1,0:T(8,128)(2,1)}, u32[]{:S(2)}) copy-start(bf16[6,768]{1,0:T(8,128)(2,1)} %param.8) | copy-start | bytes 27652
  43.0 495.0 %all-to-all-start.1 = ((bf16[64,2,64,896]{3,2,1,0:T(8,128)(2,1)}), bf16[64,2,64,896]{3,2,1,0:T(8,128)(2,1)}, u32[]{:S(2)}, u32[]{:S(2)}) async-start(bf16[64,2,64,896]{3,2,1,0:T(8,128)(2,1)} %bitcast.73), calls=%async_computation.1 | async-start | bytes 29360128 | tf_op jit(solution)/shard_map/all_to_all | solution.py:72
  49.2 495.1 %all-gather.5.cloned.1.call-start = ((), (), s32[]{:S(2)}) async-start(), calls=%async_computation.2 | async-start | bytes 7454720 | tf_op jit(solution)/shard_map/all_gather | solution.py:80
  574.4 7.4 %copy-start.2 = (f32[6,16,256,64]{2,3,1,0:T(8,128)}, f32[6,16,256,64]{2,3,1,0:T(8,128)S(1)}, u32[]{:S(2)}) copy-start(f32[6,16,256,64]{2,3,1,0:T(8,128)S(1)} %fusion.5) | copy-start | bytes 18874372
  581.8 18.1 %copy-start.1 = (bf16[64,768]{1,0:T(8,128)(2,1)S(1)}, bf16[64,768]{1,0:T(8,128)(2,1)}, u32[]{:S(2)}) copy-start(bf16[64,768]{1,0:T(8,128)(2,1)} %param.9) | copy-start | bytes 294916
Sparse Core Ops, SparseCore 0:
  52.8 128.8 all-gather.4
where the time goes:
time: 607 us
  blocking collectives  495 us (82%)
  local copies, waits for them, and re-layouts  39 us (6%)
  matrix products  38.6 us (6%)
  between operations  14.2 us (2%)
  other arithmetic  10.8 us (2%)
  starting transfers between devices  6.27 us (1%)
    all_gather x1, blocking collectives, body(): lax.all_gather(span_queries, 'keys', axis=0, tiled=True)  380 us
    all_gather x2, blocking collectives, merged(): gathered = jax.tree.map(lambda a: lax.all_gather(a, axis), part)  93 us
    all_to_all x1, blocking collectives, body(): lax.all_to_all(table, 'keys', split_axis=0, concat_axis=0, tiled=True)  22.2 us
    dot_general x1, matrix products, body(): jnp.einsum('re,tce->rtc', neighbours, lax.all_gather(kv_weight, 'keys', a...  18.7 us
    unnamed x17, local copies, waits for them, and re-layouts  16.8 us
    dot_general x1, matrix products, body(): jnp.einsum('chqk,ckhd->cqhd', weights, value_rows, preferred_element_type...  15.5 us
  transfers between devices with their start and end apart: 2, of which 0 were waited for; matrix products, arithmetic and copies ran while one was open for 3% of the time, Pallas kernels for 0%

commit v1 on v0

--- a/solution.py
+++ b/solution.py
@@ -43,7 +43,13 @@
     span_rows = neighbour_store.shape[1]
     enc_width = neighbour_store.shape[2]
     candidates = best_two(
-        row_scores(lax.all_gather(span_queries, "keys", axis=0, tiled=True), key_slab)
+        row_scores(
+            jnp.concatenate(
+                lax.all_to_all(jnp.stack([span_queries] * lax.axis_size("keys")), "keys", 0, 0),
+                axis=0,
+            ),
+            key_slab,
+        )
     )
     higher_all, runner_all = merged((candidates[:, 0], candidates[:, 1]), "keys", keep_two)
     higher = lax.dynamic_slice_in_dim(higher_all, position * own_spans, own_spans)

time: 607 us -> 570 us (0.939)
  blocking collectives: 495 us -> 441 us
  waiting for transfers between devices: 0.7 us -> 11.5 us
    all_gather x1 -> x0, blocking collectives: 380 us -> none  [body(): lax.all_gather(span_queries, 'keys', axis=0, tiled=True)]
    all_gather x2, blocking collectives: 93 us -> 419 us  [merged(): gathered = jax.tree.map(lambda a: lax.all_gather(a, axis), part)]
    all_to_all x0 -> x1, waiting for transfers between devices: none -> 10.8 us  [body(): lax.all_to_all(jnp.stack([span_queries] * lax.axis_size('keys')), 'keys',...]
    unnamed x17 -> x14, local copies, waits for them, and re-layouts: 16.8 us -> 16.6 us
  transfers between devices with their start and end apart: 2 -> 3, of which waited for: 0 -> 1; matrix products, arithmetic and copies ran while one was open for 3% -> 6% of each run, Pallas kernels for 0% -> 0%
where the time goes in v1:
time: 570 us
  blocking collectives  441 us (77%)
  local copies, waits for them, and re-layouts  40.7 us (7%)
  matrix products  38.6 us (7%)
  between operations  14.2 us (2%)
  waiting for transfers between devices  11.5 us (2%)
  starting transfers between devices  11.3 us (2%)
  other arithmetic  10.7 us (2%)
    all_gather x2, blocking collectives, merged(): gathered = jax.tree.map(lambda a: lax.all_gather(a, axis), part)  419 us
    all_to_all x1, blocking collectives, body(): lax.all_to_all(table, 'keys', split_axis=0, concat_axis=0, tiled=True)  22.2 us
    dot_general x1, matrix products, body(): jnp.einsum('re,tce->rtc', neighbours, lax.all_gather(kv_weight, 'keys', a...  18.7 us
    unnamed x14, local copies, waits for them, and re-layouts  16.6 us
    dot_general x1, matrix products, body(): jnp.einsum('chqk,ckhd->cqhd', weights, value_rows, preferred_element_type...  15.5 us
    gather x1, local copies, waits for them, and re-layouts, body(): outgoing = neighbour_store[incoming]  11.9 us
  transfers between devices with their start and end apart: 3, of which 1 were waited for; matrix products, arithmetic and copies ran while one was open for 6% of the time, Pallas kernels for 0%

profile of v1, /device:TPU:1, one launch (start us, length us, event | category | flops | bytes accessed | tf_op | source)
XLA Modules:
  0.0 569.7 jit_solution(4754678884196581791)
XLA Ops:
  7.2 0.8 copy.33
  8.5 22.2 %all_to_all.22 = s32[64,1,2]{2,1,0:T(1,128)S(1)} all-to-all(s32[64,1,2]{2,1,0:T(1,128)S(1)} %bitcast.80), channel_id=1, replica_groups=mesh['keys'=64,'seq'=4] {'keys'}, dimensions={0} | all-to-all | bytes 1024 | tf_op jit(solution)/shard_map/all_to_all | solution.py:76
  30.7 1.6 stack.14
  32.4 4.7 all-to-all-start
  37.5 11.9 %gather_fusion = bf16[128,64,896]{2,1,0:T(8,128)(2,1)} fusion(bf16[64,64,896]{2,1,0:T(8,128)(2,1)} %param.10, s32[1024]{0:T(1024)S(1)} %pad_clamp_fusion.1), kind=kCustom, calls=%fused_computation | custom fusion | bytes 29360640 | tf_op jit(solution)/shard_map/gather | solution.py:77
  49.4 10.8 %all-to-all-done = bf16[64,6,768]{2,1,0:T(8,128)(2,1)S(1)} async-done(((bf16[64,6,768]{2,1,0:T(8,128)(2,1)}), bf16[64,6,768]{2,1,0:T(8,128)(2,1)S(1)}, u32[]{:S(2)}, u32[]{:S(2)}) %all-to-all-start) | async-done | bytes 589856 | tf_op jit(solution)/shard_map/all_to_all | solution.py:48
  60.2 6.5 %all-to-all-start.2 = ((bf16[64,2,64,896]{3,2,1,0:T(8,128)(2,1)}), bf16[64,2,64,896]{3,2,1,0:T(8,128)(2,1)}, u32[]{:S(2)}, u32[]{:S(2)}) async-start(bf16[64,2,64,896]{3,2,1,0:T(8,128)(2,1)} %bitcast.72), calls=%async_computation.2 | async-start | bytes 29360128 | tf_op jit(solution)/shard_map/all_to_all | solution.py:78
  67.7 1.6 copy.44
  69.9 5.0 top_k.8
  74.9 372.3 %all-gather = f32[24576,1]{0,1:T(1,128)S(1)} all-gather(f32[384,1]{0,1:T(1,128)S(1)} %get-tuple-element.161), channel_id=2, replica_groups=mesh['keys'=64,'seq'=4] {'keys'}, dimensions={0}, use_global_device_ids=true | all-gather | bytes 99840 | tf_op jit(solution)/shard_map/all_gather | solution.py:11
  447.2 46.6 %all-gather.1 = f32[24576,1]{0,1:T(1,128)S(1)} all-gather(f32[384,1]{0,1:T(1,128)S(1)} %get-tuple-element.160), channel_id=3, replica_groups=mesh['keys'=64,'seq'=4] {'keys'}, dimensions={0}, use_global_device_ids=true | all-gather | bytes 99840 | tf_op jit(solution)/shard_map/all_gather | solution.py:11
  494.4 0.9 reduce.14
  495.2 0.9 reduce.15
  496.2 4.1 while.17
  500.9 6.3 %gather_fusion.1 = bf16[24,64,896]{2,1,0:T(8,128)(2,1)S(1)} fusion(bf16[128,64,896]{2,1,0:T(8,128)(2,1)} %bitcast.5, s32[1024]{0:T(1024)S(1)} %pad_clamp_fusion), kind=kCustom, calls=%fused_computation.1 | custom fusion | bytes 5505120 | tf_op jit(solution)/shard_map/gather | solution.py:81
  507.2 18.7 %convolution_convert_fusion = bf16[1536,2,2048]{2,0,1:T(8,128)(2,1)} fusion(bf16[1536,896,1]{1,0,2:T(8,128)(2,1)S(1)} %bitcast.77, bf16[2,2048,896]{2,1,0:T(8,128)(2,1)} %all-gather.4.cloned.1.call-done), kind=kOutput, calls=%fused_computation.6 | convolution fusion | flops 11280580608 | bytes 22675456 | tf_op jit(solution)/shard_map/re,tce->rtc/dot_general | solution.py:83
  526.0 5.3 slice_bitcast_fusion.1
  531.3 2.3 copy.43
  533.6 3.7 fusion.5
  537.3 2.4 fusion.42
  539.7 5.0 copy.45
  544.7 15.5 %fusion.16 = bf16[6,64,16,128]{3,1,2,0:T(8,128)(2,1)S(1)} fusion(bf16[6,256,16,128]{3,2,1,0:T(8,128)(2,1)} %bitcast.74, f32[6,16,64]{2,1,0:T(8,128)S(1)} %fusion.42, f32[6,16,256,64]{2,3,1,0:T(8,128)} %copy-done.2), kind=kOutput, calls=%fused_computation.24 | convolution fusion | flops 411310336 | bytes 14180352 | tf_op jit(solution)/shard_map/chqk,ckhd->cqhd/dot_general | solution.py:98
  560.3 1.0 copy.42
  561.3 1.6 copy.58
  (166 shorter events, 6.2 us)
Async XLA Ops:
  7.2 62.3 %copy-start = (bf16[64,768]{1,0:T(8,128)(2,1)S(1)}, bf16[64,768]{1,0:T(8,128)(2,1)}, u32[]{:S(2)}) copy-start(bf16[64,768]{1,0:T(8,128)(2,1)} %param.9) | copy-start | bytes 294916
  32.4 27.8 %all-to-all-start = ((bf16[64,6,768]{2,1,0:T(8,128)(2,1)}), bf16[64,6,768]{2,1,0:T(8,128)(2,1)S(1)}, u32[]{:S(2)}, u32[]{:S(2)}) async-start(bf16[64,6,768]{2,1,0:T(8,128)(2,1)} %stack.14), calls=%async_computation | async-start | bytes 1572864 | tf_op jit(solution)/shard_map/all_to_all | solution.py:48
  60.2 7.5 %copy-start.3 = (bf16[384,2048]{1,0:T(8,128)(2,1)S(1)}, bf16[384,2048]{1,0:T(8,128)(2,1)}, u32[]{:S(2)}) copy-start(bf16[384,2048]{1,0:T(8,128)(2,1)} %param.12) | copy-start | bytes 4718596
  60.2 440.7 %all-to-all-start.2 = ((bf16[64,2,64,896]{3,2,1,0:T(8,128)(2,1)}), bf16[64,2,64,896]{3,2,1,0:T(8,128)(2,1)}, u32[]{:S(2)}, u32[]{:S(2)}) async-start(bf16[64,2,64,896]{3,2,1,0:T(8,128)(2,1)} %bitcast.72), calls=%async_computation.2 | async-start | bytes 29360128 | tf_op jit(solution)/shard_map/all_to_all | solution.py:78
  66.7 440.5 %all-gather.4.cloned.1.call-start = ((), (), s32[]{:S(2)}) async-start(), calls=%async_computation.3 | async-start | bytes 7454720 | tf_op jit(solution)/shard_map/all_gather | solution.py:86
  537.3 7.4 %copy-start.2 = (f32[6,16,256,64]{2,3,1,0:T(8,128)}, f32[6,16,256,64]{2,3,1,0:T(8,128)S(1)}, u32[]{:S(2)}) copy-start(f32[6,16,256,64]{2,3,1,0:T(8,128)S(1)} %fusion.5) | copy-start | bytes 18874372
  544.7 18.1 %copy-start.1 = (bf16[64,768]{1,0:T(8,128)(2,1)S(1)}, bf16[64,768]{1,0:T(8,128)(2,1)}, u32[]{:S(2)}) copy-start(bf16[64,768]{1,0:T(8,128)(2,1)} %param.9) | copy-start | bytes 294916
Sparse Core Ops, SparseCore 0:
  70.3 128.2 all-gather.3
